TPU v7x, 512 devices: a whole 4x8x8 slice. The times are simulated.
512 devices in a mesh: tm: 8 (over y_hi, core), space: 64 (over y_lo, x, z).
Axes of the slice: x: 4, y: 8 (y_hi: 4, y_lo: 2; y = y_hi * 2 + y_lo), z: 8, core: 2. Of those that a mesh axis runs over, the one named last changes fastest.
Arguments:
- window_start: float32 [8, 64, 16, 32, 128], P('tm', 'space'), may hold values from -6 to 6
- courant_x: float32 [8, 64, 16, 32, 128], P('tm', 'space'), may hold values from -0.3 to 0.3
- courant_y: float32 [8, 64, 16, 32, 128], P('tm', 'space'), may hold values from -0.3 to 0.3
Outputs:
- window_end: float32 [8, 64, 16, 32, 128], P('tm', 'space')
All inputs are finite; a program needn't handle non-finite values.
Results may differ from a plain program's by a relative error of at most 0.00002.
Values sent between devices are 32-bit elements; how exact they have to be, the bound alone decides.
A program may use at most 64 MiB of HBM per device.

v0:
```python
import jax
import jax.numpy as jnp
from jax import lax
from jax.sharding import PartitionSpec as P

STEPS = 16
ITERS = 2
TILES_X = 8


horiz_mix = 0.06
vert_mix = 0.08
robin_coef = 0.6


def passed_along(block, axis, distance):
    devices = range(lax.axis_size(axis))
    route = [(i - distance, i) for i in devices if i - distance in devices]
    return lax.ppermute(block, axis, route)


def robin_data(inner, second):
    return inner * (1.5 * robin_coef - 1.0) + second * (1.0 - 0.5 * robin_coef)


def column_of(field, mask_col):
    return jnp.sum(jnp.where(mask_col, field, 0.0), axis=-1)


def advance(
    field,
    flow_x,
    flow_y,
    ghost_east,
    ghost_west,
    ghost_north,
    ghost_south,
    index_x,
    index_y,
    index_z,
):
    levels, rows_x, rows_y = (field.shape[-3], field.shape[-2], field.shape[-1])
    plus_x = jnp.where(
        index_x == rows_x - 1, ghost_east[..., None, :], jnp.roll(field, -1, axis=-2)
    )
    minus_x = jnp.where(index_x == 0, ghost_west[..., None, :], jnp.roll(field, 1, axis=-2))
    plus_y = jnp.where(index_y == rows_y - 1, ghost_north[..., None], jnp.roll(field, -1, axis=-1))
    minus_y = jnp.where(index_y == 0, ghost_south[..., None], jnp.roll(field, 1, axis=-1))
    plus_z = jnp.where(index_z == levels - 1, field, jnp.roll(field, -1, axis=-3))
    minus_z = jnp.where(index_z == 0, field, jnp.roll(field, 1, axis=-3))
    advect = jnp.maximum(flow_x, 0.0) * (field - minus_x) + jnp.minimum(flow_x, 0.0) * (
        plus_x - field
    )
    advect = (
        advect
        + jnp.maximum(flow_y, 0.0) * (field - minus_y)
        + jnp.minimum(flow_y, 0.0) * (plus_y - field)
    )
    spread = horiz_mix * (plus_x + minus_x + plus_y + minus_y - 4.0 * field)
    spread = spread + vert_mix * (plus_z + minus_z - 2.0 * field)
    return field - advect + spread


def run_window(
    start,
    flow_x,
    flow_y,
    data_east,
    data_west,
    data_north,
    data_south,
    has_east,
    has_west,
    has_north,
    has_south,
):
    keep_edge = 1.0 - 0.5 * robin_coef
    divisor = 1.0 + 0.5 * robin_coef
    levels, rows_x, rows_y = (start.shape[-3], start.shape[-2], start.shape[-1])
    index_z = lax.broadcasted_iota(jnp.int32, (levels, rows_x, rows_y), 0)
    index_x = lax.broadcasted_iota(jnp.int32, (levels, rows_x, rows_y), 1)
    index_y = lax.broadcasted_iota(jnp.int32, (levels, rows_x, rows_y), 2)
    first_col = index_y == 0
    second_col = index_y == 1
    last_col = index_y == rows_y - 1
    before_last = index_y == rows_y - 2

    def one_step(field, inputs):
        into_east, into_west, into_north, into_south = inputs
        south_inner = column_of(field, first_col)
        north_inner = column_of(field, last_col)
        ghost_east = has_east * (keep_edge * field[..., -1, :] + into_east) / divisor
        ghost_west = has_west * (keep_edge * field[..., 0, :] + into_west) / divisor
        ghost_north = has_north * (keep_edge * north_inner + into_north) / divisor
        ghost_south = has_south * (keep_edge * south_inner + into_south) / divisor
        edges = (
            field[..., 0, :],
            field[..., 1, :],
            field[..., -1, :],
            field[..., -2, :],
            south_inner,
            column_of(field, second_col),
            north_inner,
            column_of(field, before_last),
        )
        return (
            advance(
                field,
                flow_x,
                flow_y,
                ghost_east,
                ghost_west,
                ghost_north,
                ghost_south,
                index_x,
                index_y,
                index_z,
            ),
            edges,
        )

    return lax.scan(one_step, start, (data_east, data_west, data_north, data_south))


def body(window_start, courant_x, courant_y):
    tiles_y = lax.axis_size("space") // TILES_X
    place = lax.axis_index("space")
    tile_row = place // tiles_y
    tile_col = place % tiles_y
    has_east = (tile_row < TILES_X - 1).astype(jnp.float32)
    has_west = (tile_row > 0).astype(jnp.float32)
    has_north = (tile_col < tiles_y - 1).astype(jnp.float32)
    has_south = (tile_col > 0).astype(jnp.float32)
    first_window = lax.axis_index("tm") == 0
    lead = window_start.shape[:2]
    levels, rows_x, rows_y = (window_start.shape[2], window_start.shape[3], window_start.shape[4])
    data_x = jnp.zeros((STEPS,) + lead + (levels, rows_y), jnp.float32)
    data_y = jnp.zeros((STEPS,) + lead + (levels, rows_x), jnp.float32)
    data_east, data_west, data_north, data_south = (data_x, data_x, data_y, data_y)
    state = window_start
    ended = window_start
    for sweep in range(ITERS + 1):
        ended, edges = run_window(
            state,
            courant_x,
            courant_y,
            data_east,
            data_west,
            data_north,
            data_south,
            has_east,
            has_west,
            has_north,
            has_south,
        )
        if sweep < ITERS:
            (
                west_inner,
                west_second,
                east_inner,
                east_second,
                south_inner,
                south_second,
                north_inner,
                north_second,
            ) = edges
            offer_west = robin_data(west_inner, west_second)
            offer_east = robin_data(east_inner, east_second)
            offer_south = robin_data(south_inner, south_second)
            offer_north = robin_data(north_inner, north_second)
            from_east = passed_along(offer_west, "space", -tiles_y)
            from_west = passed_along(offer_east, "space", tiles_y)
            from_north = passed_along(offer_south, "space", -1)
            from_south = passed_along(offer_north, "space", 1)
            data_east, data_west, data_north, data_south = (
                from_east,
                from_west,
                from_north,
                from_south,
            )
            previous = passed_along(ended, "tm", 1)
            state = jnp.where(first_window, window_start, previous)
    return ended


def solution(mesh):
    in_specs = (
        P("tm", "space", None, None, None),
        P("tm", "space", None, None, None),
        P("tm", "space", None, None, None),
    )
    out_specs = P("tm", "space", None, None, None)
    return jax.shard_map(body, mesh=mesh, in_specs=in_specs, out_specs=out_specs, check_vma=False)
```

profile of v0, /device:TPU:25, one launch (start us, length us, event | category | flops | bytes accessed | tf_op | source)
XLA Modules:
  0.0 126.9 jit_solution(10993551928877644885)
XLA Ops:
  0.0 1.0 copy.37
  1.1 0.9 copy-done.1
  2.1 24.7 %while.70 = (s32[]{:T(128)}, f32[1,1,16,32,128]{4,3,2,1,0:T(8,128)S(1)}, f32[16,1,1,16,128]{4,3,2,1,0:T(8,128)S(1)}, f32[16,1,1,16,128]{4,3,2,1,0:T(8,128)S(1)},...) while((s32[]{:T(128)}, ...), condition=%wide.region_5.6_spmd.clone.clone, body=%wide.region_0.5_spmd.clone.clone.sunk | while | flops 3547138 | bytes 6738649 | solution.py:122
  3.0 0.5 fusion.132
  4.6 0.5 fusion.132
  6.1 0.5 fusion.132
  7.6 0.5 fusion.132
  9.2 0.5 fusion.132
  10.7 0.5 fusion.132
  12.3 0.5 fusion.132
  13.8 0.5 fusion.132
  15.4 0.5 fusion.132
  16.9 0.5 fusion.132
  18.4 0.5 fusion.132
  20.0 0.5 fusion.132
  21.5 0.5 fusion.132
  23.1 0.5 fusion.132
  24.6 0.5 fusion.132
  26.2 0.5 fusion.132
  26.8 12.7 %collective-permute-start.4 = (f32[16,1,1,16,32]{4,3,2,1,0:T(8,128)S(1)}, f32[16,1,1,16,32]{4,3,2,1,0:T(8,128)S(1)}, u32[]{:S(2)}, u32[]{:S(2)}) collective-permute-start(f32[16,1,1,16,32]{4,3,2,1,0:T(8,128)S(1)} %multiply_add_fusion.4), channel_id=1, source_target_pairs={{1,0},{2,1},{3,2},{4,3},{5,4},{6,5},{7,6},{8,7},{9,8},{10,9},{11,1... | collective-permute-start | bytes 98312 | tf_op jit(solution)/shard_map/ppermute | solution.py:19
  39.6 1.9 %collective-permute-start.3 = (f32[16,1,1,16,32]{4,3,2,1,0:T(8,128)S(1)}, f32[16,1,1,16,32]{4,3,2,1,0:T(8,128)S(1)}, u32[]{:S(2)}, u32[]{:S(2)}) collective-permute-start(f32[16,1,1,16,32]{4,3,2,1,0:T(8,128)S(1)} %multiply_add_fusion.5), channel_id=1, source_target_pairs={{0,1},{1,2},{2,3},{3,4},{4,5},{5,6},{6,7},{7,8},{8,9},{9,10},{10,1... | collective-permute-start | bytes 98312 | tf_op jit(solution)/shard_map/ppermute | solution.py:19
  41.5 6.3 %collective-permute-start = (f32[1,1,16,32,128]{4,3,2,1,0:T(8,128)S(1)}, f32[1,1,16,32,128]{4,3,2,1,0:T(8,128)S(1)}, u32[]{:S(2)}, u32[]{:S(2)}) collective-permute-start(f32[1,1,16,32,128]{4,3,2,1,0:T(8,128)S(1)} %get-tuple-element.537), channel_id=1, source_target_pairs={{0,64},{64,128},{128,192},{192,256},{256,320},{320,384},{384,448},... | collective-permute-start | bytes 786440 | tf_op jit(solution)/shard_map/ppermute | solution.py:19
  47.8 2.6 %collective-permute-start.2 = (f32[16,1,1,16,128]{4,3,2,1,0:T(8,128)S(1)}, f32[16,1,1,16,128]{4,3,2,1,0:T(8,128)S(1)}, u32[]{:S(2)}, u32[]{:S(2)}) collective-permute-start(f32[16,1,1,16,128]{4,3,2,1,0:T(8,128)S(1)} %multiply_add_fusion.6), channel_id=1, source_target_pairs={{8,0},{9,1},{10,2},{11,3},{12,4},{13,5},{14,6},{15,7},{16,8},{17,9... | collective-permute-start | bytes 393224 | tf_op jit(solution)/shard_map/ppermute | solution.py:19
  50.5 2.8 %collective-permute-start.1 = (f32[16,1,1,16,128]{4,3,2,1,0:T(8,128)S(1)}, f32[16,1,1,16,128]{4,3,2,1,0:T(8,128)S(1)}, u32[]{:S(2)}, u32[]{:S(2)}) collective-permute-start(f32[16,1,1,16,128]{4,3,2,1,0:T(8,128)S(1)} %multiply_add_fusion.7), channel_id=1, source_target_pairs={{0,8},{1,9},{2,10},{3,11},{4,12},{5,13},{6,14},{7,15},{8,16},{9,17... | collective-permute-start | bytes 393224 | tf_op jit(solution)/shard_map/ppermute | solution.py:19
  53.7 4.6 %collective-permute-done.1 = f32[16,1,1,16,128]{4,3,2,1,0:T(8,128)S(1)} collective-permute-done((f32[16,1,1,16,128]{4,3,2,1,0:T(8,128)S(1)}, f32[16,1,1,16,128]{4,3,2,1,0:T(8,128)S(1)}, u32[]{:S(2)}, u32[]{:S(2)}) %collective-permute-start.1) | collective-permute-done | bytes 131104 | tf_op jit(solution)/shard_map/ppermute | solution.py:19
  58.4 24.8 %while.71 = (s32[]{:T(128)}, f32[1,1,16,32,128]{4,3,2,1,0:T(8,128)S(1)}, f32[16,1,1,16,128]{4,3,2,1,0:T(8,128)S(1)}, f32[16,1,1,16,128]{4,3,2,1,0:T(8,128)S(1)},...) while((s32[]{:T(128)}, ...), condition=%wide.region_11.12_spmd.clone.clone, body=%wide.region_6.11_spmd.clone.clone.sunk | while | flops 3557378 | bytes 6759169 | solution.py:122
  83.3 6.9 %collective-permute-start.9 = (f32[16,1,1,16,32]{4,3,2,1,0:T(8,128)S(1)}, f32[16,1,1,16,32]{4,3,2,1,0:T(8,128)S(1)}, u32[]{:S(2)}, u32[]{:S(2)}) collective-permute-start(f32[16,1,1,16,32]{4,3,2,1,0:T(8,128)S(1)} %multiply_add_fusion), channel_id=1, source_target_pairs={{1,0},{2,1},{3,2},{4,3},{5,4},{6,5},{7,6},{8,7},{9,8},{10,9},{11,1... | collective-permute-start | bytes 98312 | tf_op jit(solution)/shard_map/ppermute | solution.py:19
  90.2 1.9 %collective-permute-start.8 = (f32[16,1,1,16,32]{4,3,2,1,0:T(8,128)S(1)}, f32[16,1,1,16,32]{4,3,2,1,0:T(8,128)S(1)}, u32[]{:S(2)}, u32[]{:S(2)}) collective-permute-start(f32[16,1,1,16,32]{4,3,2,1,0:T(8,128)S(1)} %multiply_add_fusion.1), channel_id=1, source_target_pairs={{0,1},{1,2},{2,3},{3,4},{4,5},{5,6},{6,7},{7,8},{8,9},{9,10},{10,1... | collective-permute-start | bytes 98312 | tf_op jit(solution)/shard_map/ppermute | solution.py:19
  92.1 4.3 %collective-permute-start.5 = (f32[1,1,16,32,128]{4,3,2,1,0:T(8,128)S(1)}, f32[1,1,16,32,128]{4,3,2,1,0:T(8,128)S(1)}, u32[]{:S(2)}, u32[]{:S(2)}) collective-permute-start(f32[1,1,16,32,128]{4,3,2,1,0:T(8,128)S(1)} %get-tuple-element.546), channel_id=1, source_target_pairs={{0,64},{64,128},{128,192},{192,256},{256,320},{320,384},{384,448},... | collective-permute-start | bytes 786440 | tf_op jit(solution)/shard_map/ppermute | solution.py:19
  96.5 1.9 %collective-permute-start.7 = (f32[16,1,1,16,128]{4,3,2,1,0:T(8,128)S(1)}, f32[16,1,1,16,128]{4,3,2,1,0:T(8,128)S(1)}, u32[]{:S(2)}, u32[]{:S(2)}) collective-permute-start(f32[16,1,1,16,128]{4,3,2,1,0:T(8,128)S(1)} %multiply_add_fusion.2), channel_id=1, source_target_pairs={{8,0},{9,1},{10,2},{11,3},{12,4},{13,5},{14,6},{15,7},{16,8},{17,9... | collective-permute-start | bytes 393224 | tf_op jit(solution)/shard_map/ppermute | solution.py:19
  98.5 4.1 %collective-permute-start.6 = (f32[16,1,1,16,128]{4,3,2,1,0:T(8,128)S(1)}, f32[16,1,1,16,128]{4,3,2,1,0:T(8,128)S(1)}, u32[]{:S(2)}, u32[]{:S(2)}) collective-permute-start(f32[16,1,1,16,128]{4,3,2,1,0:T(8,128)S(1)} %multiply_add_fusion.3), channel_id=1, source_target_pairs={{0,8},{1,9},{2,10},{3,11},{4,12},{5,13},{6,14},{7,15},{8,16},{9,17... | collective-permute-start | bytes 393224 | tf_op jit(solution)/shard_map/ppermute | solution.py:19
  103.0 3.3 %collective-permute-done.6 = f32[16,1,1,16,128]{4,3,2,1,0:T(8,128)S(1)} collective-permute-done((f32[16,1,1,16,128]{4,3,2,1,0:T(8,128)S(1)}, f32[16,1,1,16,128]{4,3,2,1,0:T(8,128)S(1)}, u32[]{:S(2)}, u32[]{:S(2)}) %collective-permute-start.6) | collective-permute-done | bytes 131104 | tf_op jit(solution)/shard_map/ppermute | solution.py:19
  106.3 19.9 %while.72 = (s32[]{:T(128)}, f32[1,1,16,32,128]{4,3,2,1,0:T(8,128)S(1)}, f32[1,1,16,32,128]{4,3,2,1,0:T(8,128)S(1)}, f32[]{:T(128)}, f32[16,1,1,16,128]{4,3,2,1,...) while((s32[]{:T(128)}, ...), condition=%wide.region_15.16_spmd.clone.clone, body=%wide.region_12.15_spmd.clone.clone.sunk | while | flops 3296258 | bytes 6132133 | solution.py:122
  107.0 0.5 fusion.149
  108.2 0.5 fusion.149
  109.5 0.5 fusion.149
  110.7 0.5 fusion.149
  112.0 0.5 fusion.149
  113.2 0.5 fusion.149
  114.5 0.5 fusion.149
  115.7 0.5 fusion.149
  116.9 0.5 fusion.149
  118.2 0.5 fusion.149
  119.4 0.5 fusion.149
  120.7 0.5 fusion.149
  121.9 0.5 fusion.149
  125.6 0.5 fusion.149
  126.2 0.7 copy-done
  (588 shorter events, 50.3 us)
Async XLA Ops:
  1.0 1.0 copy-start.1
  1.0 1.0 copy-start.2
  26.8 26.6 %collective-permute-start.4 = (f32[16,1,1,16,32]{4,3,2,1,0:T(8,128)S(1)}, f32[16,1,1,16,32]{4,3,2,1,0:T(8,128)S(1)}, u32[]{:S(2)}, u32[]{:S(2)}) collective-permute-start(f32[16,1,1,16,32]{4,3,2,1,0:T(8,128)S(1)} %multiply_add_fusion.4), channel_id=1, source_target_pairs={{1,0},{2,1},{3,2},{4,3},{5,4},{6,5},{7,6},{8,7},{9,8},{10,9},{11,1... | collective-permute-start | bytes 98312 | tf_op jit(solution)/shard_map/ppermute | solution.py:19
  39.6 13.8 %collective-permute-start.3 = (f32[16,1,1,16,32]{4,3,2,1,0:T(8,128)S(1)}, f32[16,1,1,16,32]{4,3,2,1,0:T(8,128)S(1)}, u32[]{:S(2)}, u32[]{:S(2)}) collective-permute-start(f32[16,1,1,16,32]{4,3,2,1,0:T(8,128)S(1)} %multiply_add_fusion.5), channel_id=1, source_target_pairs={{0,1},{1,2},{2,3},{3,4},{4,5},{5,6},{6,7},{7,8},{8,9},{9,10},{10,1... | collective-permute-start | bytes 98312 | tf_op jit(solution)/shard_map/ppermute | solution.py:19
  41.5 11.8 %collective-permute-start = (f32[1,1,16,32,128]{4,3,2,1,0:T(8,128)S(1)}, f32[1,1,16,32,128]{4,3,2,1,0:T(8,128)S(1)}, u32[]{:S(2)}, u32[]{:S(2)}) collective-permute-start(f32[1,1,16,32,128]{4,3,2,1,0:T(8,128)S(1)} %get-tuple-element.537), channel_id=1, source_target_pairs={{0,64},{64,128},{128,192},{192,256},{256,320},{320,384},{384,448},... | collective-permute-start | bytes 786440 | tf_op jit(solution)/shard_map/ppermute | solution.py:19
  47.8 5.5 %copy-start.3 = (f32[1,1,16,32,128]{4,3,2,1,0:T(8,128)S(1)}, f32[1,1,16,32,128]{4,3,2,1,0:T(8,128)}, u32[]{:S(2)}) copy-start(f32[1,1,16,32,128]{4,3,2,1,0:T(8,128)} %param.9) | copy-start | bytes 786436
  47.8 5.8 %collective-permute-start.2 = (f32[16,1,1,16,128]{4,3,2,1,0:T(8,128)S(1)}, f32[16,1,1,16,128]{4,3,2,1,0:T(8,128)S(1)}, u32[]{:S(2)}, u32[]{:S(2)}) collective-permute-start(f32[16,1,1,16,128]{4,3,2,1,0:T(8,128)S(1)} %multiply_add_fusion.6), channel_id=1, source_target_pairs={{8,0},{9,1},{10,2},{11,3},{12,4},{13,5},{14,6},{15,7},{16,8},{17,9... | collective-permute-start | bytes 393224 | tf_op jit(solution)/shard_map/ppermute | solution.py:19
  50.5 7.8 %collective-permute-start.1 = (f32[16,1,1,16,128]{4,3,2,1,0:T(8,128)S(1)}, f32[16,1,1,16,128]{4,3,2,1,0:T(8,128)S(1)}, u32[]{:S(2)}, u32[]{:S(2)}) collective-permute-start(f32[16,1,1,16,128]{4,3,2,1,0:T(8,128)S(1)} %multiply_add_fusion.7), channel_id=1, source_target_pairs={{0,8},{1,9},{2,10},{3,11},{4,12},{5,13},{6,14},{7,15},{8,16},{9,17... | collective-permute-start | bytes 393224 | tf_op jit(solution)/shard_map/ppermute | solution.py:19
  83.3 19.4 %collective-permute-start.9 = (f32[16,1,1,16,32]{4,3,2,1,0:T(8,128)S(1)}, f32[16,1,1,16,32]{4,3,2,1,0:T(8,128)S(1)}, u32[]{:S(2)}, u32[]{:S(2)}) collective-permute-start(f32[16,1,1,16,32]{4,3,2,1,0:T(8,128)S(1)} %multiply_add_fusion), channel_id=1, source_target_pairs={{1,0},{2,1},{3,2},{4,3},{5,4},{6,5},{7,6},{8,7},{9,8},{10,9},{11,1... | collective-permute-start | bytes 98312 | tf_op jit(solution)/shard_map/ppermute | solution.py:19
  90.2 12.5 %collective-permute-start.8 = (f32[16,1,1,16,32]{4,3,2,1,0:T(8,128)S(1)}, f32[16,1,1,16,32]{4,3,2,1,0:T(8,128)S(1)}, u32[]{:S(2)}, u32[]{:S(2)}) collective-permute-start(f32[16,1,1,16,32]{4,3,2,1,0:T(8,128)S(1)} %multiply_add_fusion.1), channel_id=1, source_target_pairs={{0,1},{1,2},{2,3},{3,4},{4,5},{5,6},{6,7},{7,8},{8,9},{9,10},{10,1... | collective-permute-start | bytes 98312 | tf_op jit(solution)/shard_map/ppermute | solution.py:19
  92.1 10.5 %collective-permute-start.5 = (f32[1,1,16,32,128]{4,3,2,1,0:T(8,128)S(1)}, f32[1,1,16,32,128]{4,3,2,1,0:T(8,128)S(1)}, u32[]{:S(2)}, u32[]{:S(2)}) collective-permute-start(f32[1,1,16,32,128]{4,3,2,1,0:T(8,128)S(1)} %get-tuple-element.546), channel_id=1, source_target_pairs={{0,64},{64,128},{128,192},{192,256},{256,320},{320,384},{384,448},... | collective-permute-start | bytes 786440 | tf_op jit(solution)/shard_map/ppermute | solution.py:19
  96.5 6.5 %collective-permute-start.7 = (f32[16,1,1,16,128]{4,3,2,1,0:T(8,128)S(1)}, f32[16,1,1,16,128]{4,3,2,1,0:T(8,128)S(1)}, u32[]{:S(2)}, u32[]{:S(2)}) collective-permute-start(f32[16,1,1,16,128]{4,3,2,1,0:T(8,128)S(1)} %multiply_add_fusion.2), channel_id=1, source_target_pairs={{8,0},{9,1},{10,2},{11,3},{12,4},{13,5},{14,6},{15,7},{16,8},{17,9... | collective-permute-start | bytes 393224 | tf_op jit(solution)/shard_map/ppermute | solution.py:19
  98.5 7.8 %collective-permute-start.6 = (f32[16,1,1,16,128]{4,3,2,1,0:T(8,128)S(1)}, f32[16,1,1,16,128]{4,3,2,1,0:T(8,128)S(1)}, u32[]{:S(2)}, u32[]{:S(2)}) collective-permute-start(f32[16,1,1,16,128]{4,3,2,1,0:T(8,128)S(1)} %multiply_add_fusion.3), channel_id=1, source_target_pairs={{0,8},{1,9},{2,10},{3,11},{4,12},{5,13},{6,14},{7,15},{8,16},{9,17... | collective-permute-start | bytes 393224 | tf_op jit(solution)/shard_map/ppermute | solution.py:19
  126.2 0.7 copy-start
where the time goes:
time: 127 us
  starting transfers between devices  45.6 us (36%)
  other arithmetic  41.4 us (33%)
  local copies, waits for them, and re-layouts  26.4 us (21%)
  waiting for transfers between devices  8.52 us (7%)
  loops' own time  4.59 us (4%)
    ppermute x10, starting transfers between devices, passed_along(): return lax.ppermute(block, axis, route)  45.6 us
    add x48, other arithmetic, advance(): return field - advect + spread  25 us
    reduce_sum x48, other arithmetic, column_of(): return jnp.sum(jnp.where(mask_col, field, 0.0), axis=-1)  14.4 us
    slice x96, local copies, waits for them, and re-layouts, advance(): jnp.roll(field, 1, axis=-1)  12.8 us
    ppermute x10, waiting for transfers between devices, passed_along(): return lax.ppermute(block, axis, route)  8.52 us
    while x32, local copies, waits for them, and re-layouts  5.04 us
    another operation x3, loops' own time, run_window(): lax.scan(one_step, start, (data_east, data_west, data_north, data_south))  4.59 us
    unnamed x9, local copies, waits for them, and re-layouts  2.6 us
  transfers between devices with their start and end apart: 10, of which 4 were waited for; matrix products, arithmetic and copies ran while one was open for 0% of the time, Pallas kernels for 0%

commit v1 on v0

v1 whole, which is shorter than its diff:
```python
import functools

import jax
import jax.numpy as jnp
from jax import lax
from jax.experimental import pallas as pl
from jax.experimental.pallas import tpu as pltpu
from jax.sharding import PartitionSpec as P

STEPS = 16
ITERS = 2
TILES_X = 8
LEVELS, ROWS_X, ROWS_Y = 16, 32, 128
PARTS = 4
BLOCKS = ROWS_X // PARTS
FIRST = 8
PADDED = ROWS_Y + 16
GROUPS = ROWS_Y // 8

HORIZ, VERT, ROBIN = 0.06, 0.08, 0.6
KEEP = (1.0 - 0.5 * ROBIN) / (1.0 + 0.5 * ROBIN)
INNER = (1.5 * ROBIN - 1.0) / (1.0 + 0.5 * ROBIN)
SECOND = (1.0 - 0.5 * ROBIN) / (1.0 + 0.5 * ROBIN)
RESCALE = VERT**STEPS

MESH = pl.DeviceIdType.MESH
f32 = jnp.float32


def lane_ids():
    return lax.broadcasted_iota(jnp.int32, (8, 128), 1)


def step(src, dst, t, coefs, ghosts, offers, has_south, has_north, scale):
    a_ref, b_ref, c_ref, d_ref, e_ref = coefs
    lane = lane_ids()
    block = lane % BLOCKS
    first_block, last_block = block == 0, block == BLOCKS - 1
    above = jnp.where(lane < 128 - BLOCKS, lane + BLOCKS, lane)
    below = jnp.where(lane >= BLOCKS, lane - BLOCKS, lane)

    south, north = src[:, FIRST, :], src[:, FIRST + ROWS_Y - 1, :]
    if offers is not None:
        east_out, west_out, south_out, north_out = offers
        south_out[pl.ds(t * PARTS, PARTS), :] = south * INNER + src[:, FIRST + 1, :] * SECOND
        north_out[pl.ds(t * PARTS, PARTS), :] = (
            north * INNER + src[:, FIRST + ROWS_Y - 2, :] * SECOND
        )
    south_ghost, north_ghost = south * (KEEP * has_south), north * (KEEP * has_north)
    if ghosts is not None:
        east_in, west_in, south_in, north_in = ghosts
        south_ghost = south_ghost + south_in[pl.ds(t * PARTS, PARTS), :]
        north_ghost = north_ghost + north_in[pl.ds(t * PARTS, PARTS), :]
    src[:, FIRST - 1, :] = south_ghost
    src[:, FIRST + ROWS_Y, :] = north_ghost

    for group in range(GROUPS):
        page, spot = group // 8, group % 8
        row = FIRST + 8 * group
        own = slice(8 * group, 8 * group + 8)
        f = [src[i, row : row + 8, :] for i in range(PARTS)]
        past_east = pltpu.roll(f[0], 127, 1)
        past_west = pltpu.roll(f[3], 1, 1)
        if ghosts is not None:
            if spot == 0:
                east_data = east_in[pl.ds(t * 16 + page * 8, 8), :]
                west_data = west_in[pl.ds(t * 16 + page * 8, 8), :]
            into_east = east_data if spot == 7 else pltpu.roll(east_data, 7 - spot, 1)
            into_west = west_data if spot == 0 else pltpu.roll(west_data, 128 - spot, 1)
        else:
            into_east = into_west = 0.0
        past_east = jnp.where(last_block, into_east, past_east)
        past_west = jnp.where(first_block, into_west, past_west)
        plus_x = f[1:] + [past_east]
        minus_x = [past_west] + f[:-1]
        for i in range(PARTS):
            plus_z = jnp.take_along_axis(f[i], above, axis=1, mode="promise_in_bounds")
            minus_z = jnp.take_along_axis(f[i], below, axis=1, mode="promise_in_bounds")
            new = (
                (a_ref[i, own, :] * plus_x[i] + b_ref[i, own, :] * minus_x[i])
                + (
                    c_ref[i, own, :] * src[i, row + 1 : row + 9, :]
                    + d_ref[i, own, :] * src[i, row - 1 : row + 7, :]
                )
                + (e_ref[i, own, :] * f[i] + (plus_z + minus_z))
            )
            if scale is not None:
                new = new * scale
            dst[i, row : row + 8, :] = new
        if offers is not None:
            east = f[2] + f[3] * (INNER / SECOND)
            west = f[1] + f[0] * (INNER / SECOND)
            if spot != 7:
                east = pltpu.roll(east, 128 - (7 - spot), 1)
            if spot != 0:
                west = pltpu.roll(west, spot, 1)
            east_pack = east if spot == 0 else jnp.where(block == spot, east, east_pack)
            west_pack = west if spot == 0 else jnp.where(block == spot, west, west_pack)
            if spot == 7:
                east_out[pl.ds(t * 16 + page * 8, 8), :] = east_pack * SECOND
                west_out[pl.ds(t * 16 + page * 8, 8), :] = west_pack * SECOND


def kernel(
    tiles_y,
    windows,
    start_hbm,
    flow_x_hbm,
    flow_y_hbm,
    out,
    raw,
    fields,
    other,
    a_ref,
    b_ref,
    c_ref,
    d_ref,
    e_ref,
    x_out,
    x_in,
    y_out,
    y_in,
    load_sem,
    send_sem,
    recv_sem,
):
    window = lax.axis_index("tm")
    place = lax.axis_index("space")
    row, col = place // tiles_y, place % tiles_y
    has_east, has_west = row < TILES_X - 1, row > 0
    has_north, has_south = col < tiles_y - 1, col > 0
    has_later, has_earlier = window < windows - 1, window > 0
    to_east, to_west = {"space": place + tiles_y}, {"space": place - tiles_y}
    to_north, to_south = {"space": place + 1}, {"space": place - 1}
    to_later, to_earlier = {"tm": window + 1}, {"tm": window - 1}

    loads = [
        pltpu.make_async_copy(ref, raw.at[k], load_sem.at[k])
        for k, ref in enumerate((flow_x_hbm, flow_y_hbm, start_hbm))
    ]
    for load in loads:
        load.start()
    barrier = pltpu.get_barrier_semaphore()
    links = (
        (to_east, has_east),
        (to_west, has_west),
        (to_north, has_north),
        (to_south, has_south),
        (to_later, has_later),
        (to_earlier, has_earlier),
    )
    count = 0
    for device, there in links:
        @pl.when(there)
        def _():
            pl.semaphore_signal(barrier, inc=1, device_id=device, device_id_type=MESH)

        count = count + there.astype(jnp.int32)

    zero_x = jnp.zeros((STEPS * 16, 128), f32)
    zero_y = jnp.zeros((STEPS * PARTS, 128), f32)
    for k in range(ITERS):
        for side, there in ((0, has_east), (1, has_west)):
            @pl.when(jnp.logical_not(there))
            def _():
                x_in[k, side] = zero_x

        for side, there in ((0, has_south), (1, has_north)):
            @pl.when(jnp.logical_not(there))
            def _():
                y_in[k, side] = zero_y

    lane = lax.broadcasted_iota(jnp.int32, (ROWS_Y, 128), 1) % BLOCKS
    east_keep = jnp.where(lane == BLOCKS - 1, has_east.astype(f32) * KEEP, 0.0)
    west_keep = jnp.where(lane == 0, has_west.astype(f32) * KEEP, 0.0)
    loads[0].wait()
    loads[1].wait()
    for i in range(PARTS):
        cx = jnp.transpose(raw[0, pl.ds(i, 128, stride=PARTS), :]) * (1.0 / VERT)
        cy = jnp.transpose(raw[1, pl.ds(i, 128, stride=PARTS), :]) * (1.0 / VERT)
        mix = HORIZ / VERT
        a = mix - jnp.minimum(cx, 0.0)
        b = mix + jnp.maximum(cx, 0.0)
        e = ((1.0 - 4.0 * HORIZ - 2.0 * VERT) / VERT - jnp.abs(cx)) - jnp.abs(cy)
        if i == 0:
            e = e + b * west_keep
        if i == PARTS - 1:
            e = e + a * east_keep
        a_ref[i] = a
        b_ref[i] = b
        c_ref[i] = mix - jnp.minimum(cy, 0.0)
        d_ref[i] = mix + jnp.maximum(cy, 0.0)
        e_ref[i] = e
    loads[2].wait()
    for i in range(PARTS):
        fields[0, i, FIRST : FIRST + ROWS_Y, :] = jnp.transpose(
            raw[2, pl.ds(i, 128, stride=PARTS), :]
        )

    @pl.when(jnp.logical_not(has_earlier))
    def _():
        for k in range(ITERS):
            fields[k + 1, :, FIRST : FIRST + ROWS_Y, :] = fields[0, :, FIRST : FIRST + ROWS_Y, :]

    coefs = (a_ref, b_ref, c_ref, d_ref, e_ref)
    south_there, north_there = has_south.astype(f32), has_north.astype(f32)
    sends = []
    for sweep in range(ITERS + 1):
        field = fields.at[sweep]
        ghosts = offers = None
        if sweep > 0:
            for copy, _, arrives in sends:
                pl.when(arrives)(copy.wait_recv)
            k = sweep - 1
            ghosts = (x_in.at[k, 0], x_in.at[k, 1], y_in.at[k, 0], y_in.at[k, 1])
        if sweep < ITERS:
            k = sweep
            offers = (x_out.at[k, 0], x_out.at[k, 1], y_out.at[k, 0], y_out.at[k, 1])

        def pair(p, last):
            t = 2 * p
            step(field, other, t, coefs, ghosts, offers, south_there, north_there, None)
            step(
                other,
                field,
                t + 1,
                coefs,
                ghosts,
                offers,
                south_there,
                north_there,
                RESCALE if last else None,
            )

        @pl.loop(0, STEPS // 2 - 1)
        def _(p):
            pair(p, False)

        pair(STEPS // 2 - 1, True)

        if sweep == 0:
            pl.semaphore_wait(barrier, count)
        if sweep < ITERS:
            k = sweep
            inside = slice(FIRST, FIRST + ROWS_Y)
            routes = (
                (field.at[:, inside, :], fields.at[sweep + 1, :, inside, :], to_later, has_later, has_earlier),
                (x_out.at[k, 0], x_in.at[k, 1], to_east, has_east, has_west),
                (x_out.at[k, 1], x_in.at[k, 0], to_west, has_west, has_east),
                (y_out.at[k, 0], y_in.at[k, 1], to_south, has_south, has_north),
                (y_out.at[k, 1], y_in.at[k, 0], to_north, has_north, has_south),
            )
            sends = []
            for n, (source, target, device, leaves, arrives) in enumerate(routes):
                copy = pltpu.make_async_remote_copy(
                    src_ref=source,
                    dst_ref=target,
                    send_sem=send_sem.at[k, n],
                    recv_sem=recv_sem.at[k, n],
                    device_id=device,
                    device_id_type=MESH,
                )
                pl.when(leaves)(copy.start)
                sends.append((copy, leaves, arrives))
            if sweep == 0:
                first_sends = sends
    out[...] = fields[ITERS, :, FIRST : FIRST + ROWS_Y, :]
    for copy, leaves, _ in first_sends + sends:
        pl.when(leaves)(copy.wait_send)


def restore(field, out):
    for i in range(PARTS):
        out[pl.ds(i, 128, stride=PARTS), :] = jnp.transpose(field[i])


def body(window_start, courant_x, courant_y):
    cells = (LEVELS * ROWS_X, ROWS_Y)
    x_data = (ITERS, 2, STEPS * 16, 128)
    y_data = (ITERS, 2, STEPS * PARTS, 128)
    whole = (PARTS, ROWS_Y, 128)
    vmem = pl.BlockSpec(memory_space=pltpu.VMEM)
    field = pl.pallas_call(
        functools.partial(kernel, lax.axis_size("space") // TILES_X, lax.axis_size("tm")),
        out_shape=jax.ShapeDtypeStruct(whole, f32),
        in_specs=[pl.BlockSpec(memory_space=pl.ANY)] * 3,
        out_specs=vmem,
        scratch_shapes=[
            pltpu.VMEM((3,) + cells, f32),
            pltpu.VMEM((ITERS + 1, PARTS, PADDED, 128), f32),
            pltpu.VMEM((PARTS, PADDED, 128), f32),
            pltpu.VMEM(whole, f32),
            pltpu.VMEM(whole, f32),
            pltpu.VMEM(whole, f32),
            pltpu.VMEM(whole, f32),
            pltpu.VMEM(whole, f32),
            pltpu.VMEM(x_data, f32),
            pltpu.VMEM(x_data, f32),
            pltpu.VMEM(y_data, f32),
            pltpu.VMEM(y_data, f32),
            pltpu.SemaphoreType.DMA((3,)),
            pltpu.SemaphoreType.DMA((ITERS, 5)),
            pltpu.SemaphoreType.DMA((ITERS, 5)),
        ],
        compiler_params=pltpu.CompilerParams(
            collective_id=0, has_side_effects=True, vmem_limit_bytes=24 << 20
        ),
    )(window_start.reshape(cells), courant_x.reshape(cells), courant_y.reshape(cells))
    ended = pl.pallas_call(
        restore,
        out_shape=jax.ShapeDtypeStruct(cells, f32),
        in_specs=[vmem],
        out_specs=vmem,
    )(field)
    return ended.reshape(window_start.shape)


def solution(mesh):
    spec = P("tm", "space", None, None, None)
    return jax.shard_map(
        body, mesh=mesh, in_specs=(spec, spec, spec), out_specs=spec, check_vma=False
    )
```

time: 127 us -> 40.3 us (0.32)
  the two profiles are of different devices: /device:TPU:25 before, /device:TPU:184 now
where the time goes in v1:
time: 40.3 us; the launch traced here: 40.1 us
  Pallas kernels  36.6 us (91%)
  local copies, waits for them, and re-layouts  3.53 us (9%)
    pallas_call x1, Pallas kernels, body(): pl.pallas_call(functools.partial(kernel, lax.axis_size('space') // TILES_...  34.8 us
    unnamed x8, local copies, waits for them, and re-layouts  3.53 us
    pallas_call x1, Pallas kernels, body(): pl.pallas_call(restore, out_shape=jax.ShapeDtypeStruct(cells, f32), in_sp...  1.79 us

profile of v1, /device:TPU:184, one launch (start us, length us, event | category | flops | bytes accessed | tf_op | source)
XLA Modules:
  0.0 40.1 jit_solution(12248574289178718981)
XLA Ops:
  0.0 0.0 copy-start.1
  0.0 0.9 %copy-done.1 = f32[1,1,16,32,128]{4,3,2,1,0:T(8,128)S(1)} copy-done((f32[1,1,16,32,128]{4,3,2,1,0:T(8,128)S(1)}, f32[1,1,16,32,128]{4,3,2,1,0:T(8,128)}, u32[]{:S(2)}) %copy-start.1) | copy-done | bytes 262168
  1.0 0.0 copy-start.2
  1.0 0.9 %copy-done.2 = f32[1,1,16,32,128]{4,3,2,1,0:T(8,128)S(1)} copy-done((f32[1,1,16,32,128]{4,3,2,1,0:T(8,128)S(1)}, f32[1,1,16,32,128]{4,3,2,1,0:T(8,128)}, u32[]{:S(2)}) %copy-start.2) | copy-done | bytes 262168
  1.9 0.0 copy-start.3
  1.9 0.9 %copy-done.3 = f32[1,1,16,32,128]{4,3,2,1,0:T(8,128)S(1)} copy-done((f32[1,1,16,32,128]{4,3,2,1,0:T(8,128)S(1)}, f32[1,1,16,32,128]{4,3,2,1,0:T(8,128)}, u32[]{:S(2)}) %copy-start.3) | copy-done | bytes 262168
  2.9 34.8 %shard_map.37.field = f32[4,128,128]{2,1,0:T(8,128)S(1)} custom-call(f32[512,128]{1,0:T(8,128)S(1)} %bitcast.4, f32[512,128]{1,0:T(8,128)S(1)} %bitcast.5, f32[512,128]{1,0:T(8,128)S(1)} %bitcast.6), custom_call_target="tpu_custom_call" | custom-call | tf_op jit(solution)/shard_map/pallas_call | solution.py:283
  37.6 0.0 copy-start
  37.6 0.7 %copy-done = f32[4,128,128]{2,1,0:T(8,128)} copy-done((f32[4,128,128]{2,1,0:T(8,128)}, f32[4,128,128]{2,1,0:T(8,128)S(1)}, u32[]{:S(2)}) %copy-start) | copy-done | bytes 262168
  38.3 1.8 %shard_map.38 = f32[512,128]{1,0:T(8,128)} custom-call(f32[4,128,128]{2,1,0:T(8,128)} %copy-done), custom_call_target="tpu_custom_call" | custom-call | tf_op jit(solution)/shard_map/pallas_call | solution.py:309
Async XLA Ops:
  0.0 0.9 %copy-start.1 = (f32[1,1,16,32,128]{4,3,2,1,0:T(8,128)S(1)}, f32[1,1,16,32,128]{4,3,2,1,0:T(8,128)}, u32[]{:S(2)}) copy-start(f32[1,1,16,32,128]{4,3,2,1,0:T(8,128)} %param.3) | copy-start | bytes 786436
  1.0 0.9 %copy-start.2 = (f32[1,1,16,32,128]{4,3,2,1,0:T(8,128)S(1)}, f32[1,1,16,32,128]{4,3,2,1,0:T(8,128)}, u32[]{:S(2)}) copy-start(f32[1,1,16,32,128]{4,3,2,1,0:T(8,128)} %param.4) | copy-start | bytes 786436
  1.9 0.9 %copy-start.3 = (f32[1,1,16,32,128]{4,3,2,1,0:T(8,128)S(1)}, f32[1,1,16,32,128]{4,3,2,1,0:T(8,128)}, u32[]{:S(2)}) copy-start(f32[1,1,16,32,128]{4,3,2,1,0:T(8,128)} %param.5) | copy-start | bytes 786436
  37.6 0.7 %copy-start = (f32[4,128,128]{2,1,0:T(8,128)}, f32[4,128,128]{2,1,0:T(8,128)S(1)}, u32[]{:S(2)}) copy-start(f32[4,128,128]{2,1,0:T(8,128)S(1)} %shard_map.37.field) | copy-start | bytes 786436

commit v2 on v1

v2 whole, which is shorter than its diff:
```python
import functools

import jax
import jax.numpy as jnp
from jax import lax
from jax.experimental import pallas as pl
from jax.experimental.pallas import tpu as pltpu
from jax.sharding import PartitionSpec as P

STEPS = 16
ITERS = 2
TILES_X = 8
LEVELS, ROWS_X, ROWS_Y = 16, 32, 128
SIDE = 4
SLABS = SIDE * SIDE
FIRST = 8
PADDED = ROWS_X + 16
GROUPS = ROWS_X // 8
HALF = STEPS // 2

HORIZ, VERT, ROBIN = 0.06, 0.08, 0.6
KEEP = (1.0 - 0.5 * ROBIN) / (1.0 + 0.5 * ROBIN)
INNER = (1.5 * ROBIN - 1.0) / (1.0 + 0.5 * ROBIN)
SECOND = (1.0 - 0.5 * ROBIN) / (1.0 + 0.5 * ROBIN)
RESCALE = VERT**STEPS

MESH = pl.DeviceIdType.MESH
f32 = jnp.float32


def lane_ids():
    return lax.broadcasted_iota(jnp.int32, (8, 128), 1)


def turn(x, by):
    return pltpu.roll(x, by % 128, 1) if by % 128 else x


def swapped(v):
    lane = lane_ids()
    low, high = lane % 2 == 0, lane % 4 < 2
    t0 = jnp.where(low, v[0], turn(v[1], 1))
    t1 = jnp.where(low, turn(v[0], -1), v[1])
    t2 = jnp.where(low, v[2], turn(v[3], 1))
    t3 = jnp.where(low, turn(v[2], -1), v[3])
    return (
        jnp.where(high, t0, turn(t2, 2)),
        jnp.where(high, t1, turn(t3, 2)),
        jnp.where(high, turn(t0, -2), t2),
        jnp.where(high, turn(t1, -2), t3),
    )


def side_rows(ref, row):
    return ref.at[pl.ds(row, SLABS, stride=PADDED), :]


def step(src, dst, t, coefs, ghosts, offers, scale):
    a_ref, b_ref, c_ref, d_ref, e_ref = coefs
    lane = lane_ids()
    north_side, south_side = lane >= 128 - SIDE, lane < SIDE
    top, bottom = lane % SIDE == SIDE - 1, lane % SIDE == 0
    south_data = lane % 8 < SIDE

    if offers is not None:
        east_out, west_out, y_out = offers
        west_out[pl.ds(t * SLABS, SLABS), :] = (
            side_rows(src, FIRST)[...] * INNER + side_rows(src, FIRST + 1)[...] * SECOND
        )
        east_out[pl.ds(t * SLABS, SLABS), :] = (
            side_rows(src, FIRST + ROWS_X - 1)[...] * INNER
            + side_rows(src, FIRST + ROWS_X - 2)[...] * SECOND
        )
    if ghosts is not None:
        east_in, west_in, south_in, north_in = ghosts
        side_rows(src, FIRST - 1)[...] = west_in[pl.ds(t * SLABS, SLABS), :]
        side_rows(src, FIRST + ROWS_X)[...] = east_in[pl.ds(t * SLABS, SLABS), :]
        both = jnp.where(
            south_data,
            turn(north_in[pl.ds(t * 8, 8), :], -SIDE),
            turn(south_in[pl.ds(t * 8, 8), :], SIDE),
        )

    packed = None
    for group in range(GROUPS):
        own = slice(8 * group, 8 * group + 8)
        f = []
        for iz in range(SIDE):
            base = [(SIDE * iz + iy) * PADDED + FIRST + 8 * group for iy in range(SIDE)]
            f.append([src[b : b + 8, :] for b in base])
        for iz in range(SIDE):
            spot = SIDE * group + iz
            ghost = 0.0 if ghosts is None else turn(both, -8 * spot - SIDE)
            past_north = jnp.where(north_side, ghost, turn(f[iz][0], -SIDE))
            past_south = jnp.where(south_side, ghost, turn(f[iz][3], SIDE))
            plus_y = f[iz][1:] + [past_north]
            minus_y = [past_south] + f[iz][:-1]
            for iy in range(SIDE):
                slab = SIDE * iz + iy
                base = slab * PADDED + FIRST + 8 * group
                if iz == SIDE - 1:
                    plus_z = jnp.where(top, f[iz][iy], turn(f[0][iy], -1))
                else:
                    plus_z = f[iz + 1][iy]
                if iz == 0:
                    minus_z = jnp.where(bottom, f[iz][iy], turn(f[SIDE - 1][iy], 1))
                else:
                    minus_z = f[iz - 1][iy]
                new = (
                    (
                        a_ref[slab, own, :] * src[base + 1 : base + 9, :]
                        + b_ref[slab, own, :] * src[base - 1 : base + 7, :]
                    )
                    + (c_ref[slab, own, :] * plus_y[iy] + d_ref[slab, own, :] * minus_y[iy])
                    + (e_ref[slab, own, :] * f[iz][iy] + (plus_z + minus_z))
                )
                if scale is not None:
                    new = new * scale
                dst[base : base + 8, :] = new
            if offers is not None:
                first = jnp.where(north_side, f[iz][3], f[iz][0])
                second = jnp.where(north_side, f[iz][2], f[iz][1])
                offer = turn(second + first * (INNER / SECOND), 8 * spot + SIDE)
                packed = offer if packed is None else jnp.where(lane // 8 == spot, offer, packed)
    if offers is not None:
        y_out[pl.ds(t * 8, 8), :] = packed * SECOND


def kernel(
    tiles_y,
    windows,
    start_hbm,
    flow_x_hbm,
    flow_y_hbm,
    out,
    raw,
    fields,
    other,
    a_ref,
    b_ref,
    c_ref,
    d_ref,
    e_ref,
    x_out,
    x_in,
    y_out,
    y_in,
    load_sem,
    send_sem,
    recv_sem,
):
    window = lax.axis_index("tm")
    place = lax.axis_index("space")
    row, col = place // tiles_y, place % tiles_y
    has_east, has_west = row < TILES_X - 1, row > 0
    has_north, has_south = col < tiles_y - 1, col > 0
    has_later, has_earlier = window < windows - 1, window > 0
    to_east, to_west = {"space": place + tiles_y}, {"space": place - tiles_y}
    to_north, to_south = {"space": place + 1}, {"space": place - 1}
    to_later, to_earlier = {"tm": window + 1}, {"tm": window - 1}

    loads = [
        pltpu.make_async_copy(ref, raw.at[k], load_sem.at[k])
        for k, ref in enumerate((flow_x_hbm, flow_y_hbm, start_hbm))
    ]
    for load in loads:
        load.start()
    barrier = pltpu.get_barrier_semaphore()
    links = (
        (to_east, has_east),
        (to_west, has_west),
        (to_north, has_north),
        (to_south, has_south),
        (to_later, has_later),
        (to_earlier, has_earlier),
    )
    count = 0
    for device, there in links:
        @pl.when(there)
        def _():
            pl.semaphore_signal(barrier, inc=1, device_id=device, device_id_type=MESH)

        count = count + there.astype(jnp.int32)

    zero_row = jnp.zeros((SLABS, 128), f32)
    for ref in (fields.at[0], other):
        side_rows(ref, FIRST - 1)[...] = zero_row
        side_rows(ref, FIRST + ROWS_X)[...] = zero_row
    zero_x = jnp.zeros((STEPS * SLABS, 128), f32)
    zero_y = jnp.zeros((STEPS * 8, 128), f32)
    for k in range(ITERS):
        for side, there in ((0, has_east), (1, has_west)):
            @pl.when(jnp.logical_not(there))
            def _():
                x_in[k, side] = zero_x

        for side, there in ((0, has_south), (1, has_north)):
            @pl.when(jnp.logical_not(there))
            def _():
                y_in[k, side] = zero_y

    lane = lane_ids()
    sub = lax.broadcasted_iota(jnp.int32, (8, 128), 0)
    east_keep = jnp.where(sub == 7, has_east.astype(f32) * KEEP, 0.0)
    west_keep = jnp.where(sub == 0, has_west.astype(f32) * KEEP, 0.0)
    north_keep = jnp.where(lane >= 128 - SIDE, has_north.astype(f32) * KEEP, 0.0)
    south_keep = jnp.where(lane < SIDE, has_south.astype(f32) * KEEP, 0.0)

    def gathered(which, group, iz):
        rows = [(SIDE * zb + iz) * ROWS_X + 8 * group for zb in range(SIDE)]
        return swapped([raw[which, r : r + 8, :] for r in rows])

    loads[0].wait()
    loads[1].wait()
    mix = HORIZ / VERT
    for group in range(GROUPS):
        own = slice(8 * group, 8 * group + 8)
        for iz in range(SIDE):
            flow_x, flow_y = gathered(0, group, iz), gathered(1, group, iz)
            for iy in range(SIDE):
                slab = SIDE * iz + iy
                cx, cy = flow_x[iy] * (1.0 / VERT), flow_y[iy] * (1.0 / VERT)
                a = mix - jnp.minimum(cx, 0.0)
                b = mix + jnp.maximum(cx, 0.0)
                c = mix - jnp.minimum(cy, 0.0)
                d = mix + jnp.maximum(cy, 0.0)
                e = ((1.0 - 4.0 * HORIZ - 2.0 * VERT) / VERT - jnp.abs(cx)) - jnp.abs(cy)
                if group == GROUPS - 1:
                    e = e + a * east_keep
                if group == 0:
                    e = e + b * west_keep
                if iy == SIDE - 1:
                    e = e + c * north_keep
                if iy == 0:
                    e = e + d * south_keep
                a_ref[slab, own, :] = a
                b_ref[slab, own, :] = b
                c_ref[slab, own, :] = c
                d_ref[slab, own, :] = d
                e_ref[slab, own, :] = e
    loads[2].wait()
    for group in range(GROUPS):
        for iz in range(SIDE):
            start = gathered(2, group, iz)
            for iy in range(SIDE):
                base = (SIDE * iz + iy) * PADDED + FIRST + 8 * group
                fields[0, base : base + 8, :] = start[iy]

    @pl.when(jnp.logical_not(has_earlier))
    def _():
        for k in range(ITERS):
            for slab in range(SLABS):
                inside = slice(slab * PADDED + FIRST, slab * PADDED + FIRST + ROWS_X)
                fields[k + 1, inside, :] = fields[0, inside, :]

    coefs = (a_ref, b_ref, c_ref, d_ref, e_ref)
    started = []

    def send(k, n, source, target, device, leaves, arrives):
        copy = pltpu.make_async_remote_copy(
            src_ref=source,
            dst_ref=target,
            send_sem=send_sem.at[k, n],
            recv_sem=recv_sem.at[k, n],
            device_id=device,
            device_id_type=MESH,
        )
        pl.when(leaves)(copy.start)
        started.append((copy, leaves))
        return copy, arrives

    def send_sides(k, part):
        x_part = pl.ds(part * HALF * SLABS, HALF * SLABS)
        y_part = pl.ds(part * HALF * 8, HALF * 8)
        n = 1 + 4 * part
        return [
            send(k, n, x_out.at[k, 0, x_part], x_in.at[k, 1, x_part], to_east, has_east, has_west),
            send(k, n + 1, x_out.at[k, 1, x_part], x_in.at[k, 0, x_part], to_west, has_west, has_east),
            send(k, n + 2, y_out.at[k, y_part], y_in.at[k, 1, y_part], to_south, has_south, has_north),
            send(k, n + 3, y_out.at[k, y_part], y_in.at[k, 0, y_part], to_north, has_north, has_south),
        ]

    def receive(copies):
        for copy, arrives in copies:
            pl.when(arrives)(copy.wait_recv)

    early = late = None
    for sweep in range(ITERS + 1):
        field = fields.at[sweep]
        ghosts = offers = None
        if sweep > 0:
            receive(early)
            k = sweep - 1
            ghosts = (x_in.at[k, 0], x_in.at[k, 1], y_in.at[k, 0], y_in.at[k, 1])
        if sweep < ITERS:
            offers = (x_out.at[sweep, 0], x_out.at[sweep, 1], y_out.at[sweep])

        def pair(p, scale=None):
            step(field, other, 2 * p, coefs, ghosts, offers, None)
            step(other, field, 2 * p + 1, coefs, ghosts, offers, scale)

        pl.loop(0, HALF // 2)(pair)
        if sweep > 0:
            receive(late)
        if sweep == 0:
            pl.semaphore_wait(barrier, count)
        if sweep < ITERS:
            early = send_sides(sweep, 0)
        pl.loop(HALF // 2, HALF - 1)(pair)
        pair(HALF - 1, RESCALE)
        if sweep < ITERS:
            inside = slice(FIRST, FIRST + ROWS_X)
            ended = field.reshape(SLABS, PADDED, 128).at[:, inside, :]
            landing = fields.at[sweep + 1].reshape(SLABS, PADDED, 128).at[:, inside, :]
            early.append(send(sweep, 0, ended, landing, to_later, has_later, has_earlier))
            late = send_sides(sweep, 1)

    for group in range(GROUPS):
        for iz in range(SIDE):
            base = [(SIDE * iz + iy) * PADDED + FIRST + 8 * group for iy in range(SIDE)]
            ended = swapped([fields[ITERS, b : b + 8, :] for b in base])
            for zb in range(SIDE):
                r = (SIDE * zb + iz) * ROWS_X + 8 * group
                out[r : r + 8, :] = ended[zb]
    for copy, leaves in started:
        pl.when(leaves)(copy.wait_send)


def body(window_start, courant_x, courant_y):
    cells = (LEVELS * ROWS_X, ROWS_Y)
    coef = pltpu.VMEM((SLABS, ROWS_X, 128), f32)
    ended = pl.pallas_call(
        functools.partial(kernel, lax.axis_size("space") // TILES_X, lax.axis_size("tm")),
        out_shape=jax.ShapeDtypeStruct(cells, f32),
        in_specs=[pl.BlockSpec(memory_space=pl.ANY)] * 3,
        out_specs=pl.BlockSpec(memory_space=pltpu.VMEM),
        scratch_shapes=[
            pltpu.VMEM((3,) + cells, f32),
            pltpu.VMEM((ITERS + 1, SLABS * PADDED, 128), f32),
            pltpu.VMEM((SLABS * PADDED, 128), f32),
            coef,
            coef,
            coef,
            coef,
            coef,
            pltpu.VMEM((ITERS, 2, STEPS * SLABS, 128), f32),
            pltpu.VMEM((ITERS, 2, STEPS * SLABS, 128), f32),
            pltpu.VMEM((ITERS, STEPS * 8, 128), f32),
            pltpu.VMEM((ITERS, 2, STEPS * 8, 128), f32),
            pltpu.SemaphoreType.DMA((3,)),
            pltpu.SemaphoreType.DMA((ITERS, 9)),
            pltpu.SemaphoreType.DMA((ITERS, 9)),
        ],
        compiler_params=pltpu.CompilerParams(
            collective_id=0, has_side_effects=True, vmem_limit_bytes=56 << 20
        ),
    )(window_start.reshape(cells), courant_x.reshape(cells), courant_y.reshape(cells))
    return ended.reshape(window_start.shape)


def solution(mesh):
    spec = P("tm", "space", None, None, None)
    return jax.shard_map(
        body, mesh=mesh, in_specs=(spec, spec, spec), out_specs=spec, check_vma=False
    )
```

time: 40.3 us -> 34.1 us (0.85)
  the two profiles are of different devices: /device:TPU:184 before, /device:TPU:440 now
where the time goes in v2:
time: 34.1 us; the launch traced here: 33.9 us
  Pallas kernels  32.3 us (95%)
  local copies, waits for them, and re-layouts  1.67 us (5%)
    pallas_call x1, Pallas kernels, body(): pl.pallas_call(functools.partial(kernel, lax.axis_size('space') // TILES_...  32.3 us
    unnamed x1, local copies, waits for them, and re-layouts  1.67 us

profile of v2, /device:TPU:440, one launch (start us, length us, event | category | flops | bytes accessed | tf_op | source)
XLA Modules:
  0.0 33.9 jit_solution(15412598750121328959)
XLA Ops:
  0.0 32.3 %shard_map.37 = f32[512,128]{1,0:T(8,128)} custom-call(f32[512,128]{1,0:T(8,128)} %bitcast.5, f32[512,128]{1,0:T(8,128)} %bitcast.6, f32[512,128]{1,0:T(8,128)} %bitcast.7), custom_call_target="tpu_custom_call" | custom-call | tf_op jit(solution)/shard_map/pallas_call | solution.py:332
  32.3 1.7 %copy.5 = f32[1,1,16,32,128]{4,3,2,1,0:T(8,128)} copy(f32[1,1,16,32,128]{4,3,2,1,0:T(8,128)} %bitcast.4) | data formatting | bytes 524288

commit v3 on v2

--- a/solution.py
+++ b/solution.py
@@ -16,7 +16,8 @@
 FIRST = 8
 PADDED = ROWS_X + 16
 GROUPS = ROWS_X // 8
-HALF = STEPS // 2
+SPAN = 4
+SPANS = STEPS // SPAN
 
 HORIZ, VERT, ROBIN = 0.06, 0.08, 0.6
 KEEP = (1.0 - 0.5 * ROBIN) / (1.0 + 0.5 * ROBIN)
@@ -148,6 +149,7 @@
     load_sem,
     send_sem,
     recv_sem,
+    field_sem,
 ):
     window = lax.axis_index("tm")
     place = lax.axis_index("space")
@@ -254,76 +256,103 @@
                 fields[k + 1, inside, :] = fields[0, inside, :]
 
     coefs = (a_ref, b_ref, c_ref, d_ref, e_ref)
-    started = []
-
-    def send(k, n, source, target, device, leaves, arrives):
+
+    def routed(source, target, sent, received, device, leaves, arrives):
         copy = pltpu.make_async_remote_copy(
             src_ref=source,
             dst_ref=target,
-            send_sem=send_sem.at[k, n],
-            recv_sem=recv_sem.at[k, n],
+            send_sem=sent,
+            recv_sem=received,
             device_id=device,
             device_id_type=MESH,
         )
-        pl.when(leaves)(copy.start)
-        started.append((copy, leaves))
-        return copy, arrives
-
-    def send_sides(k, part):
-        x_part = pl.ds(part * HALF * SLABS, HALF * SLABS)
-        y_part = pl.ds(part * HALF * 8, HALF * 8)
-        n = 1 + 4 * part
+        return copy, leaves, arrives
+
+    def sides(k, part):
+        x_part = pl.ds(part * SPAN * SLABS, SPAN * SLABS)
+        y_part = pl.ds(part * SPAN * 8, SPAN * 8)
+        routes = (
+            (x_out.at[k, 0, x_part], x_in.at[k, 1, x_part], to_east, has_east, has_west),
+            (x_out.at[k, 1, x_part], x_in.at[k, 0, x_part], to_west, has_west, has_east),
+            (y_out.at[k, y_part], y_in.at[k, 1, y_part], to_south, has_south, has_north),
+            (y_out.at[k, y_part], y_in.at[k, 0, y_part], to_north, has_north, has_south),
+        )
         return [
-            send(k, n, x_out.at[k, 0, x_part], x_in.at[k, 1, x_part], to_east, has_east, has_west),
-            send(k, n + 1, x_out.at[k, 1, x_part], x_in.at[k, 0, x_part], to_west, has_west, has_east),
-            send(k, n + 2, y_out.at[k, y_part], y_in.at[k, 1, y_part], to_south, has_south, has_north),
-            send(k, n + 3, y_out.at[k, y_part], y_in.at[k, 0, y_part], to_north, has_north, has_south),
+            routed(source, target, send_sem.at[k, part, n], recv_sem.at[k, part, n], *rest)
+            for n, (source, target, *rest) in enumerate(routes)
         ]
 
-    def receive(copies):
-        for copy, arrives in copies:
+    def ended(k):
+        inside = slice(FIRST, FIRST + ROWS_X)
+        source, target = (
+            fields.at[n].reshape(SLABS, PADDED, 128).at[:, inside, :] for n in (k, k + 1)
+        )
+        return [
+            routed(
+                source, target, field_sem.at[0, k], field_sem.at[1, k], to_later, has_later, has_earlier
+            )
+        ]
+
+    def start(copies):
+        for copy, leaves, _ in copies:
+            pl.when(leaves)(copy.start)
+
+    def arrive(copies):
+        for copy, _, arrives in copies:
             pl.when(arrives)(copy.wait_recv)
 
-    early = late = None
+    def leave(copies):
+        for copy, leaves, _ in copies:
+            pl.when(leaves)(copy.wait_send)
+
     for sweep in range(ITERS + 1):
         field = fields.at[sweep]
         ghosts = offers = None
         if sweep > 0:
-            receive(early)
             k = sweep - 1
             ghosts = (x_in.at[k, 0], x_in.at[k, 1], y_in.at[k, 0], y_in.at[k, 1])
+            arrive(ended(k))
         if sweep < ITERS:
             offers = (x_out.at[sweep, 0], x_out.at[sweep, 1], y_out.at[sweep])
 
-        def pair(p, scale=None):
-            step(field, other, 2 * p, coefs, ghosts, offers, None)
-            step(other, field, 2 * p + 1, coefs, ghosts, offers, scale)
-
-        pl.loop(0, HALF // 2)(pair)
-        if sweep > 0:
-            receive(late)
-        if sweep == 0:
-            pl.semaphore_wait(barrier, count)
+        def run(part, scale=None):
+            if sweep > 0:
+                arrive(sides(sweep - 1, part))
+            for n in range(0, SPAN, 2):
+                t = part * SPAN + n
+                last = scale if n == SPAN - 2 else None
+                step(field, other, t, coefs, ghosts, offers, None)
+                step(other, field, t + 1, coefs, ghosts, offers, last)
+
+        @pl.loop(0, SPANS - 1)
+        def _(part):
+            run(part)
+            if sweep == 0:
+                @pl.when(part == 0)
+                def _():
+                    pl.semaphore_wait(barrier, count)
+
+            if sweep < ITERS:
+                start(sides(sweep, part))
+
+        run(SPANS - 1, RESCALE)
         if sweep < ITERS:
-            early = send_sides(sweep, 0)
-        pl.loop(HALF // 2, HALF - 1)(pair)
-        pair(HALF - 1, RESCALE)
-        if sweep < ITERS:
-            inside = slice(FIRST, FIRST + ROWS_X)
-            ended = field.reshape(SLABS, PADDED, 128).at[:, inside, :]
-            landing = fields.at[sweep + 1].reshape(SLABS, PADDED, 128).at[:, inside, :]
-            early.append(send(sweep, 0, ended, landing, to_later, has_later, has_earlier))
-            late = send_sides(sweep, 1)
+            start(ended(sweep))
+            start(sides(sweep, SPANS - 1))
 
     for group in range(GROUPS):
         for iz in range(SIDE):
             base = [(SIDE * iz + iy) * PADDED + FIRST + 8 * group for iy in range(SIDE)]
-            ended = swapped([fields[ITERS, b : b + 8, :] for b in base])
+            final = swapped([fields[ITERS, b : b + 8, :] for b in base])
             for zb in range(SIDE):
                 r = (SIDE * zb + iz) * ROWS_X + 8 * group
-                out[r : r + 8, :] = ended[zb]
-    for copy, leaves in started:
-        pl.when(leaves)(copy.wait_send)
+                out[r : r + 8, :] = final[zb]
+    for k in range(ITERS):
+        leave(ended(k))
+
+        @pl.loop(0, SPANS)
+        def _(part):
+            leave(sides(k, part))
 
 
 def body(window_start, courant_x, courant_y):
@@ -332,7 +361,7 @@
     ended = pl.pallas_call(
         functools.partial(kernel, lax.axis_size("space") // TILES_X, lax.axis_size("tm")),
         out_shape=jax.ShapeDtypeStruct(cells, f32),
-        in_specs=[pl.BlockSpec(memory_space=pl.ANY)] * 3,
+        in_specs=[pl.BlockSpec(memory_space=pltpu.HBM)] * 3,
         out_specs=pl.BlockSpec(memory_space=pltpu.VMEM),
         scratch_shapes=[
             pltpu.VMEM((3,) + cells, f32),
@@ -348,8 +377,9 @@
             pltpu.VMEM((ITERS, STEPS * 8, 128), f32),
             pltpu.VMEM((ITERS, 2, STEPS * 8, 128), f32),
             pltpu.SemaphoreType.DMA((3,)),
-            pltpu.SemaphoreType.DMA((ITERS, 9)),
-            pltpu.SemaphoreType.DMA((ITERS, 9)),
+            pltpu.SemaphoreType.DMA((ITERS, SPANS, 4)),
+            pltpu.SemaphoreType.DMA((ITERS, SPANS, 4)),
+            pltpu.SemaphoreType.DMA((2, ITERS)),
         ],
         compiler_params=pltpu.CompilerParams(
             collective_id=0, has_side_effects=True, vmem_limit_bytes=56 << 20

time: 34.1 us -> 33.1 us (0.971)
  Pallas kernels: 32.3 us -> 31.2 us
    pallas_call x1, Pallas kernels: 32.3 us -> 31.2 us  [body(): pl.pallas_call(functools.partial(kernel, lax.axis_size('space') // TILES_...]
where the time goes in v3:
time: 33.1 us; the launch traced here: 32.9 us
  Pallas kernels  31.2 us (94%)
  local copies, waits for them, and re-layouts  1.67 us (5%)
    pallas_call x1, Pallas kernels, body(): pl.pallas_call(functools.partial(kernel, lax.axis_size('space') // TILES_...  31.2 us
    unnamed x1, local copies, waits for them, and re-layouts  1.67 us

profile of v3, /device:TPU:440, one launch (start us, length us, event | category | flops | bytes accessed | tf_op | source)
XLA Modules:
  0.0 32.9 jit_solution(10193302681574659099)
XLA Ops:
  0.0 31.2 %shard_map.37 = f32[512,128]{1,0:T(8,128)} custom-call(f32[512,128]{1,0:T(8,128)} %bitcast.5, f32[512,128]{1,0:T(8,128)} %bitcast.6, f32[512,128]{1,0:T(8,128)} %bitcast.7), custom_call_target="tpu_custom_call" | custom-call | tf_op jit(solution)/shard_map/pallas_call | solution.py:361
  31.2 1.7 %copy.5 = f32[1,1,16,32,128]{4,3,2,1,0:T(8,128)} copy(f32[1,1,16,32,128]{4,3,2,1,0:T(8,128)} %bitcast.4) | data formatting | bytes 524288

commit v4 on v3

--- a/solution.py
+++ b/solution.py
@@ -337,8 +337,8 @@
 
         run(SPANS - 1, RESCALE)
         if sweep < ITERS:
+            start(sides(sweep, SPANS - 1))
             start(ended(sweep))
-            start(sides(sweep, SPANS - 1))
 
     for group in range(GROUPS):
         for iz in range(SIDE):
@@ -382,7 +382,7 @@
             pltpu.SemaphoreType.DMA((2, ITERS)),
         ],
         compiler_params=pltpu.CompilerParams(
-            collective_id=0, has_side_effects=True, vmem_limit_bytes=56 << 20
+            collective_id=0, has_side_effects=True, vmem_limit_bytes=107 << 19
         ),
     )(window_start.reshape(cells), courant_x.reshape(cells), courant_y.reshape(cells))
     return ended.reshape(window_start.shape)

time: 33.1 us -> 29.4 us (0.89)
  the two profiles are of different devices: /device:TPU:440 before, /device:TPU:184 now
where the time goes in v4:
time: 29.4 us; the launch traced here: 29.2 us
  Pallas kernels  28.5 us (97%)
  local copies, waits for them, and re-layouts  0.71 us (2%)
    pallas_call x1, Pallas kernels, body(): pl.pallas_call(functools.partial(kernel, lax.axis_size('space') // TILES_...  28.5 us
    unnamed x1, local copies, waits for them, and re-layouts  0.71 us

profile of v4, /device:TPU:184, one launch (start us, length us, event | category | flops | bytes accessed | tf_op | source)
XLA Modules:
  0.0 29.2 jit_solution(14207113029590133565)
XLA Ops:
  0.0 28.5 %shard_map.37 = f32[512,128]{1,0:T(8,128)S(1)} custom-call(f32[512,128]{1,0:T(8,128)} %bitcast.5, f32[512,128]{1,0:T(8,128)} %bitcast.6, f32[512,128]{1,0:T(8,128)} %bitcast.7), custom_call_target="tpu_custom_call" | custom-call | tf_op jit(solution)/shard_map/pallas_call | solution.py:361
  28.5 0.7 %copy.5 = f32[1,1,16,32,128]{4,3,2,1,0:T(8,128)} copy(f32[1,1,16,32,128]{4,3,2,1,0:T(8,128)S(1)} %bitcast.4) | data formatting | bytes 524288

commit v5 on v4

--- a/solution.py
+++ b/solution.py
@@ -337,8 +337,9 @@
 
         run(SPANS - 1, RESCALE)
         if sweep < ITERS:
-            start(sides(sweep, SPANS - 1))
-            start(ended(sweep))
+            last = [ended(sweep), sides(sweep, SPANS - 1)]
+            for copies in last[::-1] if sweep == 0 else last:
+                start(copies)
 
     for group in range(GROUPS):
         for iz in range(SIDE):

time: 29.4 us -> 28.8 us (0.980)
  Pallas kernels: 28.5 us -> 28 us
    pallas_call x1, Pallas kernels: 28.5 us -> 28 us  [body(): pl.pallas_call(functools.partial(kernel, lax.axis_size('space') // TILES_...]
where the time goes in v5:
time: 28.8 us; the launch traced here: 28.7 us
  Pallas kernels  28 us (97%)
  local copies, waits for them, and re-layouts  0.71 us (2%)
    pallas_call x1, Pallas kernels, body(): pl.pallas_call(functools.partial(kernel, lax.axis_size('space') // TILES_...  28 us
    unnamed x1, local copies, waits for them, and re-layouts  0.71 us

profile of v5, /device:TPU:184, one launch (start us, length us, event | category | flops | bytes accessed | tf_op | source)
XLA Modules:
  0.0 28.7 jit_solution(17414909522805136382)
XLA Ops:
  0.0 28.0 %shard_map.37 = f32[512,128]{1,0:T(8,128)S(1)} custom-call(f32[512,128]{1,0:T(8,128)} %bitcast.5, f32[512,128]{1,0:T(8,128)} %bitcast.6, f32[512,128]{1,0:T(8,128)} %bitcast.7), custom_call_target="tpu_custom_call" | custom-call | tf_op jit(solution)/shard_map/pallas_call | solution.py:362
  28.0 0.7 %copy.5 = f32[1,1,16,32,128]{4,3,2,1,0:T(8,128)} copy(f32[1,1,16,32,128]{4,3,2,1,0:T(8,128)S(1)} %bitcast.4) | data formatting | bytes 524288
